TPU v7x, 32 devices: a whole 2x2x4 slice. The times are simulated.
32 devices in a mesh: occ: 4 (over y, x), vir: 8 (over z, core).
Axes of the slice: x: 2, y: 2, z: 4, core: 2. Of those that a mesh axis runs over, the one named last changes fastest.
Arguments:
- factors: bfloat16 [256, 1024, 2048], P(None, 'vir', 'occ'), may hold values from -0.125 to 0.125
- e_occ: float32 [256], replicated, may hold values from -2 to -0.3
- e_vir: float32 [1024], replicated, may hold values from 0.1 to 3
- i_sub: int32 [3], replicated, may hold values from 0 to 3
- j_row: int32 [3], replicated, may hold values from 0 to 255
Outputs:
- density: float32 [256, 1024, 2048], P(None, 'vir', 'occ')
All inputs are finite; a program needn't handle non-finite values.
Results may differ from a plain program's by a relative error of at most 0.0022.
Values may be sent and summed in bfloat16 or wider, within the bound.
No kernel may reach another device: no remote copies, remote signals or barrier semaphores. Data moves between devices by JAX's collectives and lax.ppermute only.
A program may use at most 320 MiB of HBM per device.

v0:
```python
import jax
import jax.numpy as jnp
from jax import lax
from jax.sharding import PartitionSpec as P

IBK = 16
STEPS = 3


def from_root(shard, axis, root):
    mine = lax.axis_index(axis) == root
    return lax.psum(jnp.where(mine, shard, jnp.zeros_like(shard)), axis)


def pair_terms(accumulator, row_block, energy_rows, energy_own, energy_pair, column_piece, e_vir):
    integrals = jnp.einsum(
        "iap,bp->iab", row_block, column_piece, preferred_element_type=jnp.float32
    )
    denominator = (
        energy_own[None, :, None] + e_vir[None, None, :] - energy_rows[:, None, None] - energy_pair
    )
    amplitude = (-integrals / denominator).astype(jnp.bfloat16)
    return accumulator + jnp.einsum(
        "iab,bp->iap", amplitude, column_piece, preferred_element_type=jnp.float32
    )


def shards(factors, e_occ, e_vir, i_sub, j_row):
    regrouped = lax.all_to_all(factors, "occ", split_axis=0, concat_axis=2, tiled=True)
    owned, vir_own, aux_total = regrouped.shape
    occ_rank = lax.axis_index("occ")
    vir_rank = lax.axis_index("vir")
    energy_own = lax.dynamic_slice_in_dim(e_vir, vir_rank * vir_own, vir_own, 0)
    density = jnp.zeros((owned, vir_own, aux_total), jnp.float32)
    offsets = []
    row_blocks = []
    energy_list = []
    pair_slabs = []
    pair_energies = []
    for step_index in range(STEPS):
        offset = i_sub[step_index] * IBK
        j_index = j_row[step_index]
        owner = j_index // owned
        own_slab = lax.dynamic_index_in_dim(regrouped, j_index % owned, 0, keepdims=False)
        pair_slab = from_root(own_slab, "occ", owner)
        offsets.append(offset)
        row_blocks.append(lax.dynamic_slice_in_dim(regrouped, offset, IBK, 0))
        energy_list.append(lax.dynamic_slice_in_dim(e_occ, occ_rank * owned + offset, IBK, 0))
        pair_slabs.append(pair_slab)
        pair_energies.append(e_occ[j_index])
    for step_index in range(STEPS):
        previous = lax.dynamic_slice_in_dim(density, offsets[step_index], IBK, 0)
        updated = pair_terms(
            previous,
            row_blocks[step_index],
            energy_list[step_index],
            energy_own,
            pair_energies[step_index],
            lax.all_gather(pair_slabs[step_index], "vir", axis=0, tiled=True),
            e_vir,
        )
        density = lax.dynamic_update_slice_in_dim(density, updated, offsets[step_index], 0)
    return lax.all_to_all(density, "occ", split_axis=2, concat_axis=0, tiled=True)


def solution(mesh):
    placed = (P(None, "vir", "occ"), P(), P(), P(), P())
    return jax.shard_map(
        shards, mesh=mesh, in_specs=placed, out_specs=P(None, "vir", "occ"), check_vma=False
    )
```

profile of v0, /device:TPU:0, one launch (start us, length us, event | category | flops | bytes accessed | tf_op | source)
XLA Modules:
  0.0 1660.3 jit_solution(7369690321661292340)
XLA Ops:
  6.5 9.9 all-to-all-start
  16.5 0.6 fusion.35
  24.5 355.4 %all-to-all-done = bf16[256,128,512]{2,1,0:T(8,128)(2,1)} async-done(((bf16[256,128,512]{2,1,0:T(8,128)(2,1)}), bf16[256,128,512]{2,1,0:T(8,128)(2,1)}, u32[]{:S(2)}, u32[]{:S(2)}) %all-to-all-start) | async-done | bytes 33554464 | tf_op jit(solution)/shard_map/all_to_all | solution.py:29
  379.9 37.8 %copy.12 = bf16[4,64,128,512]{3,0,2,1:T(4,128)(2,1)} copy(bf16[4,64,128,512]{3,2,1,0:T(8,128)(2,1)} %bitcast) | data formatting | bytes 67108864 | tf_op jit(solution)/shard_map/all_to_all | solution.py:29
  417.7 54.0 %all_to_all.29 = bf16[64,128,2048]{2,1,0:T(8,128)(2,1)} reshape(bf16[64,128,4,512]{3,2,1,0:T(4,128)(2,1)} %bitcast.42) | data formatting | bytes 67108864 | tf_op jit(solution)/shard_map/all_to_all | solution.py:29
  471.7 2.5 select_bitcast_fusion
  474.3 61.9 %all-reduce.3.cloned.1.call-done = (bf16[128,2048]{1,0:T(8,128)(2,1)}, bf16[128,2048]{1,0:T(8,128)(2,1)}, bf16[128,2048]{1,0:T(8,128)(2,1)}) async-done(((bf16[128,2048]{1,0:T(8,128)(2,1)}, bf16[128,2048]{1,0:T(8,128)(2,1)}, bf16[128,2048]{1,0:T(8,128)(2,1)}), (bf16[128,2048]{1,0:T(8,128)(2,1)}, bf16[128,2048]{1,0:T(8,128)(2,1)}, bf16[128,2048]{1,0:T(8,128)(2,1)})) %all-reduce.3.cloned.1.call-update) | async-done | bytes 1572880 | tf_op jit(solution)/shard_map/psum | solution.py:12
  536.3 0.7 all-gather.8.cloned.1.call-update
  537.1 0.5 all-gather.4.cloned.1.call-update
  537.6 0.6 fusion.34
  544.0 0.6 fusion.33
  544.7 0.1 broadcast_add_fusion
  544.8 40.3 %all-gather.6.cloned.1.call-done = bf16[1024,2048]{1,0:T(8,128)(2,1)} async-done(((bf16[128,2048]{1,0:T(8,128)(2,1)}), bf16[1024,2048]{1,0:T(8,128)(2,1)}) %all-gather.6.cloned.1.call-update) | async-done | bytes 4194320 | tf_op jit(solution)/shard_map/all_gather | solution.py:59
  585.1 14.5 fusion.2
  599.6 33.0 %all-gather.8.cloned.1.call-done = bf16[1024,2048]{1,0:T(8,128)(2,1)} async-done(((bf16[128,2048]{1,0:T(8,128)(2,1)}), bf16[1024,2048]{1,0:T(8,128)(2,1)}) %all-gather.8.cloned.1.call-update) | async-done | bytes 4194320 | tf_op jit(solution)/shard_map/all_gather | solution.py:59
  632.6 14.6 fusion
  647.2 33.1 %all-gather.4.cloned.1.call-done = bf16[1024,2048]{1,0:T(8,128)(2,1)} async-done(((bf16[128,2048]{1,0:T(8,128)(2,1)}), bf16[1024,2048]{1,0:T(8,128)(2,1)}) %all-gather.4.cloned.1.call-update) | async-done | bytes 4194320 | tf_op jit(solution)/shard_map/all_gather | solution.py:59
  680.3 21.6 %broadcast_in_dim.2 = f32[64,128,2048]{2,1,0:T(8,128)} broadcast(f32[]{:T(128)} %constant.66.clone.1), dimensions={} | broadcast | bytes 67108864 | tf_op jit(solution)/shard_map/broadcast_in_dim | solution.py:34
  701.8 28.0 %convolution_dynamic-update-slice_fusion = f32[64,128,2048]{2,1,0:T(8,128)} fusion(f32[64,128,2048]{2,1,0:T(8,128)} %broadcast_in_dim.2, s32[]{:T(128)S(6)} %select_n.99, bf16[1024,2048]{1,0:T(8,128)(2,1)} %all-gather.4.cloned.1.call-done, f32[]{:T(128)} %bitcast.6, f32[16]{0:T(128)S(1)} %get-tuple-element.13, f32[128,1024]{1,0:T(8,128)S(1)} %broadcast_add_fusion, ...), kind=kOutput, calls=%fused_computation.3 | convolution fusion | flops 17190354944 | bytes 34080320 | tf_op jit(solution)/shard_map/iab,bp->iap/dot_general | solution.py:23
  729.8 19.1 %add_dynamic-update-slice_fusion.1 = f32[64,128,2048]{2,1,0:T(8,128)} fusion(f32[64,128,2048]{2,1,0:T(8,128)} %convolution_dynamic-update-slice_fusion, s32[]{:T(128)S(6)} %select_n.109, f32[16,128,1024]{2,1,0:T(8,128)} %fusion.2, bf16[1024,2048]{1,0:T(8,128)(2,1)} %all-gather.6.cloned.1.call-done, f32[]{:T(128)} %bitcast.11, f32[16]{0:T(128)S(1)} %get-tuple-element.12, ...), kind=kOutput, calls=%fused_computation.2 | convolution fusion | flops 8604614656 | bytes 46662212 | tf_op jit(solution)/shard_map/iab,bp->iap/dot_general | solution.py:23
  748.9 19.3 %add_dynamic-update-slice_fusion = f32[64,128,2048]{2,1,0:T(8,128)} fusion(f32[64,128,2048]{2,1,0:T(8,128)} %add_dynamic-update-slice_fusion.1, s32[]{:T(128)S(6)} %select_n.118, f32[16,128,1024]{2,1,0:T(8,128)} %fusion, bf16[1024,2048]{1,0:T(8,128)(2,1)} %all-gather.8.cloned.1.call-done, f32[]{:T(128)} %bitcast.16, f32[16]{0:T(128)S(1)} %get-tuple-element.11, ...), kind=kOutput, calls=%fused_computation.1 | convolution fusion | flops 8604614656 | bytes 46662212 | tf_op jit(solution)/shard_map/iab,bp->iap/dot_general | solution.py:23
  768.2 63.4 %copy.9 = f32[64,128,2048]{1,0,2:T(8,128)} copy(f32[64,128,2048]{2,1,0:T(8,128)} %add_dynamic-update-slice_fusion) | data formatting | bytes 134217728 | tf_op jit(solution)/shard_map/dynamic_update_slice | solution.py:62
  831.6 755.0 %all_to_all.36 = f32[64,128,2048]{1,0,2:T(8,128)} all-to-all(f32[64,128,2048]{1,0,2:T(8,128)} %copy.9), channel_id=1, replica_groups=mesh['occ'=4,'vir'=8] {'occ'}, dimensions={2} | all-to-all | bytes 134217728 | tf_op jit(solution)/shard_map/all_to_all | solution.py:63
  1586.6 67.1 %copy.10 = f32[4,64,128,512]{3,2,1,0:T(8,128)} copy(f32[4,64,128,512]{2,1,3,0:T(8,128)} %bitcast.18) | data formatting | bytes 134217728 | tf_op jit(solution)/shard_map/all_to_all | solution.py:63
  (16 shorter events, 0.4 us)
Async XLA Ops:
  6.5 9.9 copy-start.1
  6.5 373.4 %all-to-all-start = ((bf16[256,128,512]{2,1,0:T(8,128)(2,1)}), bf16[256,128,512]{2,1,0:T(8,128)(2,1)}, u32[]{:S(2)}, u32[]{:S(2)}) async-start(bf16[256,128,512]{2,1,0:T(8,128)(2,1)} %param.5), calls=%async_computation | async-start | bytes 67108864 | tf_op jit(solution)/shard_map/all_to_all | solution.py:29
  16.4 519.8 %all-reduce.3.cloned.1.call-start = ((), (), s32[]{:S(2)}) async-start(), calls=%async_computation.5 | async-start | bytes 3145728 | tf_op jit(solution)/shard_map/psum | solution.py:12
  417.7 119.9 %copy-start.2 = (s32[3]{0:T(128)S(1)}, s32[3]{0:T(128)}, u32[]{:S(2)}) copy-start(s32[3]{0:T(128)} %param.8) | copy-start | bytes 40
  417.7 126.2 %copy-start.3 = (f32[1024]{0:T(1024)S(1)}, f32[1024]{0:T(1024)}, u32[]{:S(2)}) copy-start(f32[1024]{0:T(1024)} %param.7) | copy-start | bytes 12292
  417.7 126.3 %copy-start = (f32[256]{0:T(256)S(1)}, f32[256]{0:T(256)}, u32[]{:S(2)}) copy-start(f32[256]{0:T(256)} %param.6) | copy-start | bytes 3076
  474.3 110.9 %all-gather.6.cloned.1.call-start = ((), (), s32[]{:S(2)}) async-start(), calls=%async_computation.3 | async-start | bytes 4718592 | tf_op jit(solution)/shard_map/all_gather | solution.py:59
  536.3 96.3 %all-gather.8.cloned.1.call-start = ((), (), s32[]{:S(2)}) async-start(), calls=%async_computation.4 | async-start | bytes 4718592 | tf_op jit(solution)/shard_map/all_gather | solution.py:59
  537.0 143.3 %all-gather.4.cloned.1.call-start = ((), (), s32[]{:S(2)}) async-start(), calls=%async_computation.2 | async-start | bytes 4718592 | tf_op jit(solution)/shard_map/all_gather | solution.py:59
Sparse Core Ops, SparseCore 0:
  474.4 61.8 all-reduce.2
  537.9 47.1 all-gather.5
  586.8 45.7 all-gather.7
  634.1 46.0 all-gather.3
where the time goes:
time: 1670 us; the launch traced here: 1660 us
  blocking collectives  755 us (45%)
  waiting for transfers between devices  525 us (31%)
  local copies, waits for them, and re-layouts  246 us (15%)
  matrix products  95.4 us (6%)
  between operations  26.3 us (2%)
    all_to_all x1, blocking collectives, shards(): lax.all_to_all(density, 'occ', split_axis=2, concat_axis=0, tiled=True)  755 us
    all_to_all x1, waiting for transfers between devices, shards(): lax.all_to_all(factors, 'occ', split_axis=0, concat_axis=2, tiled=True)  355 us
    all_gather x3, waiting for transfers between devices, shards(): lax.all_gather(pair_slabs[step_index], 'vir', axis=0, tiled=True)  106 us
    all_to_all x2, local copies, waits for them, and re-layouts, shards(): lax.all_to_all(factors, 'occ', split_axis=0, concat_axis=2, tiled=True)  91.8 us
    all_to_all x1, local copies, waits for them, and re-layouts, shards(): lax.all_to_all(density, 'occ', split_axis=2, concat_axis=0, tiled=True)  67.1 us
    dot_general x3, matrix products, pair_terms(): jnp.einsum('iab,bp->iap', amplitude, column_piece, preferred_element_type...  66.4 us
    dynamic_update_slice x1, local copies, waits for them, and re-layouts, shards(): lax.dynamic_update_slice_in_dim(density, updated, offsets[step_index], 0)  63.4 us
    psum x1, waiting for transfers between devices, from_root(): return lax.psum(jnp.where(mine, shard, jnp.zeros_like(shard)), axis)  61.9 us
  transfers between devices with their start and end apart: 5, of which 5 were waited for; matrix products, arithmetic and copies ran while one was open for 2% of the time, Pallas kernels for 0%

commit v1 on v0

v1 whole, which is shorter than its diff:
```python
import functools

import jax
import jax.numpy as jnp
from jax import lax
from jax.experimental import pallas as pl
from jax.experimental.pallas import tpu as pltpu
from jax.sharding import PartitionSpec as P

IBK = 16
CODE_MAX = 32767.0
LARGEST_MIN = 1e-33
TAIL = 16


def exchange(piece, partner):
    size = lax.axis_size("occ")
    return lax.ppermute(piece, "occ", [(r, r ^ partner) for r in range(size)])


def after(values, *earlier):
    return lax.optimization_barrier((values, earlier))[0]


def swapped(pieces):
    return {m: exchange(piece, m) for m, piece in pieces.items()}


def rounds_of(n_occ, turn):
    masks = range(1, n_occ)
    near = tuple(m for m in masks if m & (m - 1) == 0)
    rounds = [near] + [(m,) for m in masks if m not in near]
    return rounds if turn % 2 else rounds[::-1]


def pair_kernel(n_steps, n_occ, entry, skip, row_entries, plan_ref, e_occ_ref, own_ref, *refs):
    row_refs = (own_ref,) + refs[: n_occ - 1]
    refs = refs[n_occ - 1 :]
    e_own_ref, e_vir_ref = refs[:2]
    slab_refs = refs[2 : 2 + n_steps]
    own_out = refs[3 + n_steps]
    code_refs = refs[4 + n_steps : 3 + n_steps + n_occ]
    amp_ref, power_ref = refs[3 + n_steps + n_occ :]
    ib, vir_own, aux_own = own_ref.shape
    rows = ib * vir_own
    vir_total = e_vir_ref.shape[1]
    block = pl.program_id(0)
    wide = min(256, vir_total)

    for n in range(n_steps):

        def integrals_of(c, carry, n=n):
            at = pl.ds(pl.multiple_of(c * wide, wide), wide)
            integrals = None
            for m in range(n_occ):
                term = lax.dot_general(
                    row_refs[m][...].reshape(rows, aux_own),
                    slab_refs[n][at, m * aux_own : (m + 1) * aux_own],
                    (((1,), (1,)), ((), ())),
                    preferred_element_type=jnp.float32,
                )
                integrals = term if integrals is None else integrals + term
            e_pair = e_occ_ref[plan_ref[row_entries[n]]]
            for k in range(ib):
                shift = e_occ_ref[plan_ref[entry] + skip + block * ib + k] + e_pair
                part = integrals[k * vir_own : (k + 1) * vir_own]
                denominator = e_own_ref[...] + (e_vir_ref[:, at] - shift)
                amp_ref[n, k * vir_own : (k + 1) * vir_own, at] = (-part / denominator).astype(jnp.bfloat16)
            return carry

        lax.fori_loop(0, vir_total // wide, integrals_of, 0)

    tall = min(256, rows)
    held = tall // vir_own

    def density_of(r, carry):
        at = pl.ds(pl.multiple_of(r * tall, tall), tall)
        for m in range(n_occ):
            density = None
            for n in range(n_steps):
                term = jnp.dot(
                    amp_ref[n, at, :],
                    slab_refs[n][:, m * aux_own : (m + 1) * aux_own],
                    preferred_element_type=jnp.float32,
                )
                density = term if density is None else density + term
            if m == 0:
                own_out[pl.ds(r * held, held)] = density.reshape(held, vir_own, aux_own)
            else:
                largest = jnp.maximum(jnp.max(jnp.abs(density), axis=1, keepdims=True), LARGEST_MIN)
                power = jnp.floor(jnp.log2(CODE_MAX / largest))
                codes = jnp.clip(jnp.round(density * jnp.exp2(power)), -CODE_MAX, CODE_MAX)
                at_all = pl.ds(pl.multiple_of(block * rows + r * tall, tall), tall)
                code_refs[m - 1][at_all, :] = codes.astype(jnp.int32).astype(jnp.int16)
                power_ref[m - 1, pl.ds(block * ib + r * held, held), :] = power.reshape(held, vir_own)
        return carry

    lax.fori_loop(0, rows // tall, density_of, 0)

    @pl.when(block == pl.num_programs(0) - 1)
    def _():
        for m in range(1, n_occ):
            last = code_refs[m - 1].shape[0] - TAIL
            powers = power_ref[m - 1].astype(jnp.int32).astype(jnp.int16)
            code_refs[m - 1][last:, :] = jnp.zeros((TAIL, aux_own), jnp.int16)
            code_refs[m - 1][last:, :vir_own] = powers


def blocks_of(count, vir_own):
    return max(1, min(count, 512 // vir_own))


def picked(factors, plan, entries, count):
    _, vir_own, aux_own = factors.shape
    ib = min(4, count)

    def body(plan_ref, *refs):
        half = len(refs) // 2
        for source, target in zip(refs[:half], refs[half:]):
            target[...] = source[...]

    def source_of(entry, skip):
        return pl.BlockSpec((ib, vir_own, aux_own), lambda i, plan: (plan[entry] // ib + skip // ib + i, 0, 0))

    return pl.pallas_call(
        body,
        grid_spec=pltpu.PrefetchScalarGridSpec(
            num_scalar_prefetch=1,
            grid=(count // ib,),
            in_specs=[source_of(*entry) for entry in entries],
            out_specs=[pl.BlockSpec((ib, vir_own, aux_own), lambda i, plan: (i, 0, 0))] * len(entries),
        ),
        out_shape=[jax.ShapeDtypeStruct((count, vir_own, aux_own), factors.dtype)] * len(entries),
        compiler_params=pltpu.CompilerParams(vmem_limit_bytes=48 * 2**20),
        cost_estimate=pl.CostEstimate(
            flops=0, bytes_accessed=4 * len(entries) * count * vir_own * aux_own, transcendentals=0
        ),
    )(plan, *([factors] * len(entries)))


def pair_block(density, factors, plan, e_occ, entry, skip, row_entries, received, slabs, members, e_own, e_vir):
    n_steps, n_occ = len(members), len(received) + 1
    count, vir_own, aux_own = received[0].shape
    vir_total, aux_total = slabs.shape[0], n_occ * aux_own
    ib = blocks_of(count, vir_own)
    rows = ib * vir_own
    whole = pl.BlockSpec(memory_space=pltpu.VMEM)
    piece = pl.BlockSpec((ib, vir_own, aux_own), lambda i, plan: (i, 0, 0))
    own = pl.BlockSpec((ib, vir_own, aux_own), lambda i, plan: (plan[entry] // ib + skip // ib + i, 0, 0))
    coded = (count * vir_own + TAIL, aux_own)
    flops = 4 * count * vir_own * vir_total * aux_total * n_steps
    outs = pl.pallas_call(
        functools.partial(pair_kernel, n_steps, n_occ, entry, skip, row_entries),
        grid_spec=pltpu.PrefetchScalarGridSpec(
            num_scalar_prefetch=1,
            grid=(count // ib,),
            in_specs=[pl.BlockSpec(memory_space=pltpu.SMEM), own]
            + [piece] * (n_occ - 1)
            + [whole] * 2
            + [pl.BlockSpec((vir_total, aux_total), lambda i, plan, s=s: (0, s)) for s in members]
            + [pl.BlockSpec(memory_space=pl.ANY)],
            out_specs=[own] + [pl.BlockSpec(coded, lambda i, plan: (0, 0))] * (n_occ - 1),
            scratch_shapes=[
                pltpu.VMEM((n_steps, rows, vir_total), jnp.bfloat16),
                pltpu.VMEM((n_occ - 1, TAIL, vir_own), jnp.float32),
            ],
        ),
        out_shape=[jax.ShapeDtypeStruct(density.shape, jnp.float32)]
        + [jax.ShapeDtypeStruct(coded, jnp.int16)] * (n_occ - 1),
        input_output_aliases={n_occ + n_steps + 4: 0},
        compiler_params=pltpu.CompilerParams(vmem_limit_bytes=48 * 2**20),
        cost_estimate=pl.CostEstimate(flops=flops, bytes_accessed=16 * 2**20, transcendentals=0),
    )(plan, e_occ, factors, *received, e_own[:, None], e_vir[None, :], *([slabs] * n_steps), density)
    return outs[0], outs[1:]


def decoded(density, plan, entry, skip, codes, count):
    _, vir_own, aux_own = density.shape
    ib = blocks_of(count, vir_own)

    def body(plan_ref, code_ref, power_ref, density_ref, out_ref):
        block = pl.program_id(0)
        powers = power_ref[...].astype(jnp.float32)[:, :vir_own]
        for k in range(ib):
            at = jax.lax.broadcasted_iota(jnp.int32, powers.shape, 0) == block * ib + k
            power = jnp.sum(jnp.where(at, powers, 0.0), axis=0, keepdims=True)
            scale = jnp.exp2(-jnp.broadcast_to(power, (8, vir_own)).T[:, :1])
            part = code_ref[k * vir_own : (k + 1) * vir_own, :].astype(jnp.float32)
            out_ref[k] = part * scale

    return pl.pallas_call(
        body,
        grid_spec=pltpu.PrefetchScalarGridSpec(
            num_scalar_prefetch=1,
            grid=(count // ib,),
            in_specs=[
                pl.BlockSpec((ib * vir_own, aux_own), lambda i, plan: (i, 0)),
                pl.BlockSpec((TAIL, aux_own), lambda i, plan: (count * vir_own // TAIL, 0)),
                pl.BlockSpec(memory_space=pl.ANY),
            ],
            out_specs=pl.BlockSpec(
                (ib, vir_own, aux_own), lambda i, plan: (plan[entry] // ib + skip // ib + i, 0, 0)
            ),
        ),
        out_shape=jax.ShapeDtypeStruct(density.shape, jnp.float32),
        input_output_aliases={3: 0},
        compiler_params=pltpu.CompilerParams(vmem_limit_bytes=24 * 2**20),
        cost_estimate=pl.CostEstimate(
            flops=0, bytes_accessed=6 * count * vir_own * aux_own, transcendentals=0
        ),
    )(plan, codes, codes, density)


def planned(sizes, factors, e_occ, e_vir, e_own, plan):
    n_occ = lax.axis_size("occ")
    steps = sum(sizes)

    def entry_of(step, partner):
        return step * n_occ + partner

    def row_entry_of(step):
        return steps * n_occ + step

    cuts = 2 if len(sizes) == 1 else 1
    count = IBK // cuts
    starts = [sum(sizes[:u]) for u in range(len(sizes))]
    items = [(u, cut * count) for u in range(len(sizes)) for cut in range(cuts)]
    pair_own = picked(factors, plan, [(row_entry_of(s), 0) for s in range(steps)], 1)
    pair_got = swapped({m: jnp.concatenate(pair_own, axis=0) for m in range(1, n_occ)})
    density = None
    received = []
    for turn, (u, skip) in enumerate(items):
        at = plan if turn == 0 else after(plan, density)
        got = {}
        for partners in rounds_of(n_occ, turn):
            entries = [(entry_of(starts[u], m), skip) for m in partners]
            pieces = dict(zip(partners, picked(factors, at, entries, count)))
            if turn == 0:
                pair_got = after(pair_got, pieces)
            got.update(swapped(pieces))
        received.append([got[m] for m in range(1, n_occ)])
        if turn == 0:
            density = jnp.full(factors.shape, after(jnp.float32(0.0), pair_got[1]), jnp.float32)

    pair_rows = jnp.concatenate(
        [part for s in range(steps) for part in [pair_own[s][0]] + [pair_got[m][s] for m in range(1, n_occ)]],
        axis=1,
    )
    slabs = lax.all_gather(pair_rows, "vir", axis=0, tiled=True)

    coded = []
    for (u, skip), pieces in zip(items, received):
        members = range(starts[u], starts[u] + sizes[u])
        density, codes = pair_block(
            density,
            factors,
            plan,
            e_occ,
            entry_of(starts[u], 0),
            skip,
            [row_entry_of(s) for s in members],
            pieces,
            slabs,
            members,
            e_own,
            e_vir,
        )
        coded.append(codes)

    for turn, ((u, skip), codes) in enumerate(zip(items, coded), len(items)):
        for partners in rounds_of(n_occ, turn):
            got = swapped({m: codes[m - 1] for m in partners})
            for m in partners:
                density = decoded(density, plan, entry_of(starts[u], m), skip, got[m], count)
    return density


def partitions(total, largest):
    if total == 0:
        return [()]
    return [rest + (p,) for p in range(min(total, largest), 0, -1) for rest in partitions(total - p, p)]


def plan_kernel(sizes_list, owned, n_occ, sub_ref, row_ref, plan_ref, branch_ref):
    steps = sub_ref.shape[0]
    subs = [sub_ref[s] for s in range(steps)]

    def total(terms):
        return functools.reduce(lambda a, b: a + b, terms)

    def chosen(holds, value=1):
        return jnp.where(holds, jnp.int32(value), jnp.int32(0))

    shared = [total([chosen(subs[s] == subs[t]) for t in range(steps)]) for s in range(steps)]
    keys = [(shared[s] * (owned // IBK) + subs[s]) * steps + s for s in range(steps)]
    places = [total([chosen(keys[t] < keys[s]) for t in range(steps)]) for s in range(steps)]
    me = lax.axis_index("occ")
    found = []
    for p in range(steps):
        sub = total([chosen(places[s] == p, subs[s]) for s in range(steps)])
        plan_ref[steps * n_occ + p] = total([chosen(places[s] == p, row_ref[s]) for s in range(steps)])
        found.append(total([chosen(places[s] == p, shared[s]) for s in range(steps)]))
        for m in range(n_occ):
            plan_ref[p * n_occ + m] = (me ^ m) * owned + sub * IBK
    branch = jnp.int32(0)
    for b, sizes in enumerate(sizes_list):
        wanted = sum(([p] * p for p in sizes), [])
        missed = total([chosen(have != want) for have, want in zip(found, wanted)])
        branch = jnp.where(missed == 0, jnp.int32(b), branch)
    branch_ref[0] = branch


def shards(factors, e_occ, e_vir, i_sub, j_row):
    vir_own = factors.shape[1]
    n_occ = lax.axis_size("occ")
    owned = factors.shape[0] // n_occ
    steps = i_sub.shape[0]
    sizes_list = [p for p in partitions(steps, steps) if len(p) <= owned // IBK]
    sizes_list.sort(key=lambda sizes: abs(len(sizes) - 2))
    scalars = pl.BlockSpec(memory_space=pltpu.SMEM)
    plan, branch = pl.pallas_call(
        functools.partial(plan_kernel, sizes_list, owned, n_occ),
        in_specs=[scalars, scalars],
        out_specs=[scalars, scalars],
        out_shape=[
            jax.ShapeDtypeStruct((steps * (n_occ + 1),), jnp.int32),
            jax.ShapeDtypeStruct((1,), jnp.int32),
        ],
    )(i_sub, j_row)
    e_own = lax.dynamic_slice_in_dim(e_vir, lax.axis_index("vir") * vir_own, vir_own, 0)
    return lax.switch(
        branch[0],
        [functools.partial(planned, sizes) for sizes in sizes_list],
        factors,
        e_occ,
        e_vir,
        e_own,
        plan,
    )


def solution(mesh):
    placed = (P(None, "vir", "occ"), P(), P(), P(), P())
    return jax.shard_map(
        shards, mesh=mesh, in_specs=placed, out_specs=P(None, "vir", "occ"), check_vma=False
    )
```

time: 1670 us -> 411 us (0.25)
  blocking collectives: 755 us -> 0 us
  waiting for transfers between devices: 525 us -> 224 us
  local copies, waits for them, and re-layouts: 246 us -> 23.1 us
  Pallas kernels: 0 us -> 129 us
  matrix products: 95.4 us -> 0 us
    all_to_all x1 -> x0, blocking collectives: 755 us -> none  [shards(): lax.all_to_all(density, 'occ', split_axis=2, concat_axis=0, tiled=True)]
    all_to_all x1 -> x0, waiting for transfers between devices: 355 us -> none  [shards(): lax.all_to_all(factors, 'occ', split_axis=0, concat_axis=2, tiled=True)]
    ppermute x0 -> x15, waiting for transfers between devices: none -> 201 us  [exchange(): return lax.ppermute(piece, 'occ', [(r, r ^ partner) for r in range(size)])]
    all_to_all x3 -> x0, local copies, waits for them, and re-layouts: 159 us -> none  [the longest x2 91.8 us: shards(): lax.all_to_all(factors, 'occ', split_axis=0, concat_axis=2, tiled=True)]
    pallas_call x0 -> x14, Pallas kernels: none -> 129 us  [the longest x2 82.7 us: pair_block(): pl.pallas_call(functools.partial(pair_kernel, n_steps, n_occ, entry, skip...]
    dot_general x5 -> x0, matrix products: 95.4 us -> none  [the longest x3 66.4 us: pair_terms(): jnp.einsum('iab,bp->iap', amplitude, column_piece, preferred_element_type...]
    all_gather x3 -> x1, waiting for transfers between devices: 106 us -> 22.5 us  [planned(): slabs = lax.all_gather(pair_rows, 'vir', axis=0, tiled=True)]
    dynamic_update_slice x1 -> x0, local copies, waits for them, and re-layouts: 63.4 us -> none  [shards(): lax.dynamic_update_slice_in_dim(density, updated, offsets[step_index], 0)]
  transfers between devices with their start and end apart: 5 -> 16, of which waited for: 5 -> 10; matrix products, arithmetic and copies ran while one was open for 2% -> 5% of each run, Pallas kernels for 0% -> 30%
where the time goes in v1:
time: 411 us; the launch traced here: 410 us
  waiting for transfers between devices  224 us (55%)
  Pallas kernels  129 us (31%)
  local copies, waits for them, and re-layouts  23.1 us (6%)
  starting transfers between devices  19.6 us (5%)
  between operations  14 us (3%)
    ppermute x15, waiting for transfers between devices, exchange(): return lax.ppermute(piece, 'occ', [(r, r ^ partner) for r in range(size)])  201 us
    pallas_call x2, Pallas kernels, pair_block(): pl.pallas_call(functools.partial(pair_kernel, n_steps, n_occ, entry, skip...  82.7 us
    pallas_call x6, Pallas kernels, decoded(): pl.pallas_call(body, grid_spec=pltpu.PrefetchScalarGridSpec(num_scalar_pr...  23.9 us
    all_gather x1, waiting for transfers between devices, planned(): slabs = lax.all_gather(pair_rows, 'vir', axis=0, tiled=True)  22.5 us
    broadcast_in_dim x1, local copies, waits for them, and re-layouts, planned(): jnp.full(factors.shape, after(jnp.float32(0.0), pair_got[1]), jnp.float32)  21.6 us
    pallas_call x5, Pallas kernels, picked(): pl.pallas_call(body, grid_spec=pltpu.PrefetchScalarGridSpec(num_scalar_pr...  21.4 us
    ppermute x15, starting transfers between devices, exchange(): return lax.ppermute(piece, 'occ', [(r, r ^ partner) for r in range(size)])  19.5 us
  transfers between devices with their start and end apart: 16, of which 10 were waited for; matrix products, arithmetic and copies ran while one was open for 5% of the time, Pallas kernels for 30%

profile of v1, /device:TPU:0, one launch (start us, length us, event | category | flops | bytes accessed | tf_op | source)
XLA Modules:
  0.0 410.1 jit_solution(7898118448189350983)
XLA Ops:
  8.5 394.7 %conditional.1 = (f32[256,128,512]{2,1,0:T(8,128)}) conditional(s32[]{:T(128)} %bitcast.42, (s32[15]{0:T(128)S(1)}, bf16[256,128,512]{2,1,0:T(8,128)(2,1)}, f32[1024]{0:T(1024)}, f32[1024]{0:T(1024)}, f32[256]{0:T(256)}, /*index=5*/s32[]{:T(128)}, (), (), (), ()) %tuple.26, (s32[15]{0:T(128)S(1)}, bf16[256,128,512]{2,1,0:T(8,128)(2,1)}, ...), branch_computations={%region_0.0_spmd, %region_1.0_spmd, %region_2.0_spmd} | conditional | flops 51539607552 | bytes 438393792 | solution.py:331
  8.6 1.6 branch_0_fun.13
  10.2 4.0 collective-permute-start.2
  14.8 4.4 %branch_0_fun.14 = bf16[16,128,512]{2,1,0:T(8,128)(2,1)} custom-call(s32[15]{0:T(128)S(1)} %get-tuple-element.52.plan_ref, bf16[256,128,512]{2,1,0:T(8,128)(2,1)} %get-tuple-element.146.refs_0_.refs_1_.refs_2_.own_ref), custom_call_target="tpu_custom_call" | custom-call | bytes 4194304 | tf_op jit(solution)/shard_map/cond/branch_0_fun/pallas_call | solution.py:125
  19.2 5.2 %branch_0_fun.15 = (bf16[16,128,512]{2,1,0:T(8,128)(2,1)}, bf16[16,128,512]{2,1,0:T(8,128)(2,1)}) custom-call(s32[15]{0:T(128)S(1)} %get-tuple-element.52.plan_ref, bf16[256,128,512]{2,1,0:T(8,128)(2,1)} %get-tuple-element.146.refs_0_.refs_1_.refs_2_.own_ref, bf16[256,128,512]{2,1,0:T(8,128)(2,1)} %get-tuple-element.146.refs_0_.refs_1_.refs_2_.own_ref), custom_call_target="tpu_custom_call" | custom-call | bytes 8388608 | tf_op jit(solution)/shard_map/cond/branch_0_fun/pallas_call | solution.py:125
  24.5 7.2 %collective-permute-done.1 = bf16[3,128,512]{2,1,0:T(8,128)(2,1)S(1)} collective-permute-done((bf16[3,128,512]{2,1,0:T(8,128)(2,1)S(1)}, bf16[3,128,512]{2,1,0:T(8,128)(2,1)S(1)}, u32[]{:S(2)}, u32[]{:S(2)}) %collective-permute-start.1) | collective-permute-done | bytes 393248 | tf_op jit(solution)/shard_map/cond/branch_0_fun/ppermute | solution.py:18
  36.9 4.4 %branch_0_fun.17 = bf16[16,128,512]{2,1,0:T(8,128)(2,1)} custom-call(s32[15]{0:T(128)S(1)} %get-tuple-element.52.plan_ref, bf16[256,128,512]{2,1,0:T(8,128)(2,1)} %get-tuple-element.146.refs_0_.refs_1_.refs_2_.own_ref), custom_call_target="tpu_custom_call" | custom-call | bytes 4194304 | tf_op jit(solution)/shard_map/cond/branch_0_fun/pallas_call | solution.py:125
  41.3 5.8 %branch_0_fun.16 = (bf16[16,128,512]{2,1,0:T(8,128)(2,1)}, bf16[16,128,512]{2,1,0:T(8,128)(2,1)}) custom-call(s32[15]{0:T(128)S(1)} %get-tuple-element.52.plan_ref, bf16[256,128,512]{2,1,0:T(8,128)(2,1)} %get-tuple-element.146.refs_0_.refs_1_.refs_2_.own_ref, bf16[256,128,512]{2,1,0:T(8,128)(2,1)} %get-tuple-element.146.refs_0_.refs_1_.refs_2_.own_ref), custom_call_target="tpu_custom_call" | custom-call | bytes 8388608 | tf_op jit(solution)/shard_map/cond/branch_0_fun/pallas_call | solution.py:125
  49.9 33.3 %collective-permute-done.8.refs_2_ = bf16[16,128,512]{2,1,0:T(8,128)(2,1)} collective-permute-done((bf16[16,128,512]{2,1,0:T(8,128)(2,1)}, bf16[16,128,512]{2,1,0:T(8,128)(2,1)}, u32[]{:S(2)}, u32[]{:S(2)}) %collective-permute-start.8) | collective-permute-done | bytes 2097184 | tf_op jit(solution)/shard_map/cond/branch_0_fun/ppermute | solution.py:18
  84.8 43.3 %collective-permute-done.6.refs_0_ = bf16[16,128,512]{2,1,0:T(8,128)(2,1)} collective-permute-done((bf16[16,128,512]{2,1,0:T(8,128)(2,1)}, bf16[16,128,512]{2,1,0:T(8,128)(2,1)}, u32[]{:S(2)}, u32[]{:S(2)}) %collective-permute-start.6) | collective-permute-done | bytes 2097184 | tf_op jit(solution)/shard_map/cond/branch_0_fun/ppermute | solution.py:18
  128.2 22.5 %all-gather.4.cloned.1.call-done.refs_5_.refs_6_ = bf16[1024,6144]{1,0:T(8,128)(2,1)} async-done(((bf16[128,6144]{1,0:T(8,128)(2,1)}), bf16[1024,6144]{1,0:T(8,128)(2,1)}) %all-gather.4.cloned.1.call-update) | async-done | bytes 12582928 | tf_op jit(solution)/shard_map/cond/branch_0_fun/all_gather | solution.py:249
  150.7 21.6 %broadcast_in_dim.14.clone.refs_6_ = f32[256,128,512]{2,1,0:T(8,128)} broadcast(f32[]{:T(128)} %constant.3.clone), dimensions={} | broadcast | bytes 67108864 | tf_op jit(solution)/shard_map/cond/branch_0_fun/broadcast_in_dim | solution.py:243
  172.3 30.4 %branch_0_fun.18 = (f32[256,128,512]{2,1,0:T(8,128)}, s16[2064,512]{1,0:T(8,128)(2,1)}, s16[2064,512]{1,0:T(8,128)(2,1)}, s16[2064,512]{1,0:T(8,128)(2,1)}) custom-call(s32[15]{0:T(128)S(1)} %get-tuple-element.52.plan_ref, f32[256]{0:T(256)S(1)} %copy-done.8, ...), custom_call_target="tpu_custom_call", output_to_operand_aliasing={{0}: (9, {})} | custom-call | flops 17179869184 | bytes 16777216 | tf_op jit(solution)/shard_map/cond/branch_0_fun/pallas_call | solution.py:152
  206.2 11.8 %collective-permute-done.3.refs_0_ = bf16[16,128,512]{2,1,0:T(8,128)(2,1)S(1)} collective-permute-done((bf16[16,128,512]{2,1,0:T(8,128)(2,1)}, bf16[16,128,512]{2,1,0:T(8,128)(2,1)S(1)}, u32[]{:S(2)}, u32[]{:S(2)}) %collective-permute-start.3) | collective-permute-done | bytes 2097184 | tf_op jit(solution)/shard_map/cond/branch_0_fun/ppermute | solution.py:18
  217.9 52.3 %branch_0_fun.19 = (f32[256,128,512]{2,1,0:T(8,128)}, s16[2064,512]{1,0:T(8,128)(2,1)}, s16[2064,512]{1,0:T(8,128)(2,1)}, s16[2064,512]{1,0:T(8,128)(2,1)}) custom-call(s32[15]{0:T(128)S(1)} %get-tuple-element.52.plan_ref, f32[256]{0:T(256)S(1)} %copy-done.8, ...), custom_call_target="tpu_custom_call", output_to_operand_aliasing={{0}: (10, {})} | custom-call | flops 34359738368 | bytes 16777216 | tf_op jit(solution)/shard_map/cond/branch_0_fun/pallas_call | solution.py:152
  272.3 36.3 %collective-permute-done.14.code_ref.power_ref = s16[2064,512]{1,0:T(8,128)(2,1)S(1)} collective-permute-done((s16[2064,512]{1,0:T(8,128)(2,1)}, s16[2064,512]{1,0:T(8,128)(2,1)S(1)}, u32[]{:S(2)}, u32[]{:S(2)}) %collective-permute-start.14) | collective-permute-done | bytes 2113568 | tf_op jit(solution)/shard_map/cond/branch_0_fun/ppermute | solution.py:18
  310.2 3.4 branch_0_fun.20.density_ref
  313.6 3.4 branch_0_fun.21.density_ref
  317.0 3.4 branch_0_fun.22.density_ref
  320.4 33.4 %collective-permute-done.11.code_ref.power_ref = s16[2064,512]{1,0:T(8,128)(2,1)S(1)} collective-permute-done((s16[2064,512]{1,0:T(8,128)(2,1)}, s16[2064,512]{1,0:T(8,128)(2,1)S(1)}, u32[]{:S(2)}, u32[]{:S(2)}) %collective-permute-start.11) | collective-permute-done | bytes 2113568 | tf_op jit(solution)/shard_map/cond/branch_0_fun/ppermute | solution.py:18
  353.8 3.4 branch_0_fun.23.density_ref
  357.3 5.2 %branch_0_fun.24.density_ref = f32[256,128,512]{2,1,0:T(8,128)} custom-call(s32[15]{0:T(128)S(1)} %get-tuple-element.52.plan_ref, s16[2064,512]{1,0:T(8,128)(2,1)} %collective-permute-done.10.code_ref.power_ref, s16[2064,512]{1,0:T(8,128)(2,1)} %collective-permute-done.10.code_ref.power_ref, ...), custom_call_target="tpu_custom_call", output_to_operand_aliasing={{}: (3, {})} | custom-call | bytes 6291456 | tf_op jit(solution)/shard_map/cond/branch_0_fun/pallas_call | solution.py:191
  362.4 35.6 %collective-permute-done.9.code_ref.power_ref = s16[2064,512]{1,0:T(8,128)(2,1)} collective-permute-done((s16[2064,512]{1,0:T(8,128)(2,1)}, s16[2064,512]{1,0:T(8,128)(2,1)}, u32[]{:S(2)}, u32[]{:S(2)}) %collective-permute-start.9) | collective-permute-done | bytes 2113568 | tf_op jit(solution)/shard_map/cond/branch_0_fun/ppermute | solution.py:18
  398.1 5.2 %branch_0_fun.25 = f32[256,128,512]{2,1,0:T(8,128)} custom-call(s32[15]{0:T(128)S(1)} %get-tuple-element.52.plan_ref, s16[2064,512]{1,0:T(8,128)(2,1)} %collective-permute-done.9.code_ref.power_ref, s16[2064,512]{1,0:T(8,128)(2,1)} %collective-permute-done.9.code_ref.power_ref, f32[256,128,512]{2,1,0:T(8,128)} %branch_0_fun.24.density_ref), custom_call_target="tpu_custom_call", output_to_operand_aliasing={{}: (3, {})} | custom-call | bytes 6291456 | tf_op jit(solution)/shard_map/cond/branch_0_fun/pallas_call | solution.py:191
  (48 shorter events, 18.9 us)
Async XLA Ops:
  8.5 142.2 %all-gather.4.cloned.1.call-start = ((), (), s32[]{:S(2)}) async-start(), calls=%async_computation | async-start | bytes 14155776 | tf_op jit(solution)/shard_map/cond/branch_0_fun/all_gather | solution.py:249
  10.2 14.2 %collective-permute-start.2 = (bf16[3,128,512]{2,1,0:T(8,128)(2,1)S(1)}, bf16[3,128,512]{2,1,0:T(8,128)(2,1)S(1)}, u32[]{:S(2)}, u32[]{:S(2)}) collective-permute-start(bf16[3,128,512]{2,1,0:T(8,128)(2,1)S(1)} %constant_dynamic-update-slice_fusion), channel_id=1, source_target_pairs={{0,24},{8,16},{16,8},{24,0},{1,25},{9,17},{17,9},{25,1},{2,26},{10... | collective-permute-start | bytes 1179656 | tf_op jit(solution)/shard_map/cond/branch_0_fun/ppermute | solution.py:18
  14.2 17.5 %collective-permute-start.1 = (bf16[3,128,512]{2,1,0:T(8,128)(2,1)S(1)}, bf16[3,128,512]{2,1,0:T(8,128)(2,1)S(1)}, u32[]{:S(2)}, u32[]{:S(2)}) collective-permute-start(bf16[3,128,512]{2,1,0:T(8,128)(2,1)S(1)} %constant_dynamic-update-slice_fusion), channel_id=1, source_target_pairs={{0,16},{8,24},{16,0},{24,8},{1,17},{9,25},{17,1},{25,9},{2,18},{10... | collective-permute-start | bytes 1179656 | tf_op jit(solution)/shard_map/cond/branch_0_fun/ppermute | solution.py:18
  14.7 17.3 %collective-permute-start = (bf16[3,128,512]{2,1,0:T(8,128)(2,1)S(1)}, bf16[3,128,512]{2,1,0:T(8,128)(2,1)S(1)}, u32[]{:S(2)}, u32[]{:S(2)}) collective-permute-start(bf16[3,128,512]{2,1,0:T(8,128)(2,1)S(1)} %constant_dynamic-update-slice_fusion), channel_id=1, source_target_pairs={{0,8},{8,0},{16,24},{24,16},{1,9},{9,1},{17,25},{25,17},{2,10},{10... | collective-permute-start | bytes 1179656 | tf_op jit(solution)/shard_map/cond/branch_0_fun/ppermute | solution.py:18
  32.2 1.1 copy-start.2
  33.4 49.9 %collective-permute-start.8 = (bf16[16,128,512]{2,1,0:T(8,128)(2,1)}, bf16[16,128,512]{2,1,0:T(8,128)(2,1)}, u32[]{:S(2)}, u32[]{:S(2)}) collective-permute-start(bf16[16,128,512]{2,1,0:T(8,128)(2,1)} %branch_0_fun.14), channel_id=1, source_target_pairs={{0,24},{8,16},{16,8},{24,0},{1,25},{9,17},{17,9},{25,1},{2,26},{10... | collective-permute-start | bytes 6291464 | tf_op jit(solution)/shard_map/cond/branch_0_fun/ppermute | solution.py:18
  35.0 93.1 %collective-permute-start.6 = (bf16[16,128,512]{2,1,0:T(8,128)(2,1)}, bf16[16,128,512]{2,1,0:T(8,128)(2,1)}, u32[]{:S(2)}, u32[]{:S(2)}) collective-permute-start(bf16[16,128,512]{2,1,0:T(8,128)(2,1)} %get-tuple-element.48), channel_id=1, source_target_pairs={{0,8},{8,0},{16,24},{24,16},{1,9},{9,1},{17,25},{25,17},{2,10},{10... | collective-permute-start | bytes 6291464 | tf_op jit(solution)/shard_map/cond/branch_0_fun/ppermute | solution.py:18
  36.3 91.9 %collective-permute-start.7 = (bf16[16,128,512]{2,1,0:T(8,128)(2,1)}, bf16[16,128,512]{2,1,0:T(8,128)(2,1)}, u32[]{:S(2)}, u32[]{:S(2)}) collective-permute-start(bf16[16,128,512]{2,1,0:T(8,128)(2,1)} %get-tuple-element.49), channel_id=1, source_target_pairs={{0,16},{8,24},{16,0},{24,8},{1,17},{9,25},{17,1},{25,9},{2,18},{10... | collective-permute-start | bytes 6291464 | tf_op jit(solution)/shard_map/cond/branch_0_fun/ppermute | solution.py:18
  41.3 43.3 %copy-start.5 = (f32[1024]{0:T(1024)S(1)}, f32[1024]{0:T(1024)}, u32[]{:S(2)}) copy-start(f32[1024]{0:T(1024)} %get-tuple-element.56) | copy-start | bytes 12292 | tf_op jit(solution)/shard_map/cond
  47.1 158.5 %collective-permute-start.5 = (bf16[16,128,512]{2,1,0:T(8,128)(2,1)}, bf16[16,128,512]{2,1,0:T(8,128)(2,1)}, u32[]{:S(2)}, u32[]{:S(2)}) collective-permute-start(bf16[16,128,512]{2,1,0:T(8,128)(2,1)} %branch_0_fun.17), channel_id=1, source_target_pairs={{0,24},{8,16},{16,8},{24,0},{1,25},{9,17},{17,9},{25,1},{2,26},{10... | collective-permute-start | bytes 6291464 | tf_op jit(solution)/shard_map/cond/branch_0_fun/ppermute | solution.py:18
  48.3 169.6 %collective-permute-start.3 = (bf16[16,128,512]{2,1,0:T(8,128)(2,1)}, bf16[16,128,512]{2,1,0:T(8,128)(2,1)S(1)}, u32[]{:S(2)}, u32[]{:S(2)}) collective-permute-start(bf16[16,128,512]{2,1,0:T(8,128)(2,1)} %get-tuple-element.53), channel_id=1, source_target_pairs={{0,8},{8,0},{16,24},{24,16},{1,9},{9,1},{17,25},{25,17},{2,10},{10... | collective-permute-start | bytes 6291464 | tf_op jit(solution)/shard_map/cond/branch_0_fun/ppermute | solution.py:18
  83.2 134.7 %collective-permute-start.4 = (bf16[16,128,512]{2,1,0:T(8,128)(2,1)}, bf16[16,128,512]{2,1,0:T(8,128)(2,1)}, u32[]{:S(2)}, u32[]{:S(2)}) collective-permute-start(bf16[16,128,512]{2,1,0:T(8,128)(2,1)} %get-tuple-element.54), channel_id=1, source_target_pairs={{0,16},{8,24},{16,0},{24,8},{1,17},{9,25},{17,1},{25,9},{2,18},{10... | collective-permute-start | bytes 6291464 | tf_op jit(solution)/shard_map/cond/branch_0_fun/ppermute | solution.py:18
  150.7 21.6 %copy-start.8 = (f32[256]{0:T(256)S(1)}, f32[256]{0:T(256)}, u32[]{:S(2)}) copy-start(f32[256]{0:T(256)} %get-tuple-element.158.e_occ_ref) | copy-start | bytes 3076 | tf_op jit(solution)/shard_map/cond
  202.7 114.3 %collective-permute-start.12 = (s16[2064,512]{1,0:T(8,128)(2,1)}, s16[2064,512]{1,0:T(8,128)(2,1)S(1)}, u32[]{:S(2)}, u32[]{:S(2)}) collective-permute-start(s16[2064,512]{1,0:T(8,128)(2,1)} %get-tuple-element.63), channel_id=1, source_target_pairs={{0,16},{8,24},{16,0},{24,8},{1,17},{9,25},{17,1},{25,9},{2,18},{10... | collective-permute-start | bytes 6340616 | tf_op jit(solution)/shard_map/cond/branch_0_fun/ppermute | solution.py:18
  204.1 109.5 %collective-permute-start.13 = (s16[2064,512]{1,0:T(8,128)(2,1)}, s16[2064,512]{1,0:T(8,128)(2,1)S(1)}, u32[]{:S(2)}, u32[]{:S(2)}) collective-permute-start(s16[2064,512]{1,0:T(8,128)(2,1)} %get-tuple-element.64), channel_id=1, source_target_pairs={{0,8},{8,0},{16,24},{24,16},{1,9},{9,1},{17,25},{25,17},{2,10},{10... | collective-permute-start | bytes 6340616 | tf_op jit(solution)/shard_map/cond/branch_0_fun/ppermute | solution.py:18
  205.6 103.0 %collective-permute-start.14 = (s16[2064,512]{1,0:T(8,128)(2,1)}, s16[2064,512]{1,0:T(8,128)(2,1)S(1)}, u32[]{:S(2)}, u32[]{:S(2)}) collective-permute-start(s16[2064,512]{1,0:T(8,128)(2,1)} %get-tuple-element.65), channel_id=1, source_target_pairs={{0,24},{8,16},{16,8},{24,0},{1,25},{9,17},{17,9},{25,1},{2,26},{10... | collective-permute-start | bytes 6340616 | tf_op jit(solution)/shard_map/cond/branch_0_fun/ppermute | solution.py:18
  270.2 83.6 %collective-permute-start.11 = (s16[2064,512]{1,0:T(8,128)(2,1)}, s16[2064,512]{1,0:T(8,128)(2,1)S(1)}, u32[]{:S(2)}, u32[]{:S(2)}) collective-permute-start(s16[2064,512]{1,0:T(8,128)(2,1)} %get-tuple-element.62), channel_id=1, source_target_pairs={{0,8},{8,0},{16,24},{24,16},{1,9},{9,1},{17,25},{25,17},{2,10},{10... | collective-permute-start | bytes 6340616 | tf_op jit(solution)/shard_map/cond/branch_0_fun/ppermute | solution.py:18
  271.0 86.3 %collective-permute-start.10 = (s16[2064,512]{1,0:T(8,128)(2,1)}, s16[2064,512]{1,0:T(8,128)(2,1)}, u32[]{:S(2)}, u32[]{:S(2)}) collective-permute-start(s16[2064,512]{1,0:T(8,128)(2,1)} %get-tuple-element.61), channel_id=1, source_target_pairs={{0,16},{8,24},{16,0},{24,8},{1,17},{9,25},{17,1},{25,9},{2,18},{10... | collective-permute-start | bytes 6340616 | tf_op jit(solution)/shard_map/cond/branch_0_fun/ppermute | solution.py:18
  308.6 89.4 %collective-permute-start.9 = (s16[2064,512]{1,0:T(8,128)(2,1)}, s16[2064,512]{1,0:T(8,128)(2,1)}, u32[]{:S(2)}, u32[]{:S(2)}) collective-permute-start(s16[2064,512]{1,0:T(8,128)(2,1)} %get-tuple-element.60), channel_id=1, source_target_pairs={{0,24},{8,16},{16,8},{24,0},{1,25},{9,17},{17,9},{25,1},{2,26},{10... | collective-permute-start | bytes 6340616 | tf_op jit(solution)/shard_map/cond/branch_0_fun/ppermute | solution.py:18
Sparse Core Ops, SparseCore 0:
  33.5 117.1 all-gather.3
